TPU v7x, 256 devices: a whole 4x4x8 slice. The times are simulated.
256 devices in a mesh: row: 8 (over y, z_hi), col: 32 (over x, z_lo, core).
Axes of the slice: x: 4, y: 4, z: 8 (z_hi: 2, z_lo: 4; z = z_hi * 4 + z_lo), core: 2. Of those that a mesh axis runs over, the one named last changes fastest.
Arguments:
- query: bfloat16 [32768, 256], P(('row', 'col')), may hold values from -30 to 30
- key: bfloat16 [32768, 128], P(('row', 'col')), may hold values from -6 to 6
- value: bfloat16 [32768, 128], P(('row', 'col')), may hold values from -6 to 6
- out_grad: bfloat16 [32768, 256], P(('row', 'col')), may hold values from -6 to 6
- attn_out: bfloat16 [32768, 256], P(('row', 'col')), may hold values from -6 to 6
- lse: float32 [32768, 2], P(('row', 'col')), may hold values from -40 to 400, as said below
- positions: int32 [32768], replicated, may hold values from 0 to 32767, as said below
Outputs:
- query_grad: bfloat16 [32768, 256], P(('row', 'col'))
- key_grad: bfloat16 [32768, 128], P(('row', 'col'))
- value_grad: bfloat16 [32768, 128], P(('row', 'col'))
Inputs may be any that keep to these rules, and one draw needn't show every extreme that they name: A permutation of 0 to 32767; each aligned run of 64 stored rows holds 64 consecutive positions in rising order. `lse`: the forward pass's log of the sum over allowed keys of exp(scores) for each row and query head.
All inputs are finite; a program needn't handle non-finite values.
Results may differ from a plain program's by a relative error of at most 0.011.
Values may be sent and summed in bfloat16 or wider, within the bound.
A program may use at most 64 MiB of HBM per device.

v0:
```python
import math

import jax
import jax.numpy as jnp
from jax import lax
from jax.sharding import PartitionSpec as P

HEAD_DIM = 128
GROUP = 2
KV_HEADS = 1


def local_positions(positions, axis_name):
    grid = positions.reshape(lax.axis_size("row"), lax.axis_size("col"), -1)
    if axis_name == "col":
        return lax.dynamic_index_in_dim(grid, lax.axis_index("row"), 0, keepdims=False).reshape(-1)
    return lax.dynamic_index_in_dim(grid, lax.axis_index("col"), 1, keepdims=False).reshape(-1)


def split_blocks(array, size):
    return array.reshape((array.shape[0] // size, size) + array.shape[1:])


def row_delta(grads, outputs):
    rows = grads.shape[0]
    wide_grads = grads.astype(jnp.float32).reshape(rows, KV_HEADS * GROUP, HEAD_DIM)
    wide_outs = outputs.astype(jnp.float32).reshape(rows, KV_HEADS * GROUP, HEAD_DIM)
    return jnp.sum(wide_grads * wide_outs, -1)


def gradients(q_all, do_all, k_all, v_all, q_pos, k_pos, lse_rows, delta_rows):
    scale = 1.0 / math.sqrt(HEAD_DIM)
    rows = q_all.shape[0]
    k_rows = k_all.shape[0]
    q_size = math.gcd(rows, 512)
    k_size = math.gcd(k_rows, 512)
    q_count = rows // q_size
    k_count = k_rows // k_size
    q_all = q_all.reshape(rows, KV_HEADS, GROUP, HEAD_DIM)
    do_all = do_all.reshape(rows, KV_HEADS, GROUP, HEAD_DIM)
    k_all = k_all.reshape(k_rows, KV_HEADS, HEAD_DIM)
    v_all = v_all.reshape(k_rows, KV_HEADS, HEAD_DIM)
    delta_blocks = jnp.transpose(delta_rows.reshape(q_count, q_size, KV_HEADS, GROUP), (0, 2, 3, 1))
    lse_blocks = jnp.transpose(lse_rows.reshape(q_count, q_size, KV_HEADS, GROUP), (0, 2, 3, 1))
    k_blocks = split_blocks(k_all, k_size)
    v_blocks = split_blocks(v_all, k_size)
    kpos_blocks = split_blocks(k_pos, k_size)

    def per_query(carry, pieces):
        key_acc, value_acc = carry
        q_block, do_block, q_place, lse_block, delta_block = pieces

        def per_key(q_grad, items):
            k_block, v_block, k_place, key_part, value_part = items
            allowed = k_place[None, :] <= q_place[:, None]
            scores = (
                jnp.einsum("qgcd,kgd->gcqk", q_block, k_block, preferred_element_type=jnp.float32)
                * scale
            )
            probs = jnp.where(allowed[None, None], jnp.exp(scores - lse_block[..., None]), 0.0)
            dprobs = jnp.einsum(
                "qgcd,kgd->gcqk", do_block, v_block, preferred_element_type=jnp.float32
            )
            dscores = (probs * (dprobs - delta_block[..., None])).astype(jnp.bfloat16)
            probs_low = probs.astype(jnp.bfloat16)
            q_grad = q_grad + jnp.einsum(
                "gcqk,kgd->qgcd", dscores, k_block, preferred_element_type=jnp.float32
            )
            key_part = key_part + jnp.einsum(
                "gcqk,qgcd->kgd", dscores, q_block, preferred_element_type=jnp.float32
            )
            value_part = value_part + jnp.einsum(
                "gcqk,qgcd->kgd", probs_low, do_block, preferred_element_type=jnp.float32
            )
            return (q_grad, (key_part, value_part))

        start = jnp.zeros((q_size, KV_HEADS, GROUP, HEAD_DIM), jnp.float32)
        q_grad, updated = lax.scan(
            per_key, start, (k_blocks, v_blocks, kpos_blocks, key_acc, value_acc)
        )
        return (updated, q_grad * scale)

    zeros = jnp.zeros((k_count, k_size, KV_HEADS, HEAD_DIM), jnp.float32)
    pieces = (
        split_blocks(q_all, q_size),
        split_blocks(do_all, q_size),
        split_blocks(q_pos, q_size),
        lse_blocks,
        delta_blocks,
    )
    (key_acc, value_acc), q_grads = lax.scan(per_query, (zeros, zeros), pieces)
    q_grads = q_grads.reshape(rows, KV_HEADS * GROUP * HEAD_DIM)
    key_acc = key_acc.reshape(k_rows, KV_HEADS * HEAD_DIM) * scale
    value_acc = value_acc.reshape(k_rows, KV_HEADS * HEAD_DIM)
    return (q_grads, key_acc, value_acc)


def body(query, key, value, out_grad, attn_out, lse, positions):
    delta = row_delta(out_grad, attn_out)
    q_all, do_all, lse_all, delta_all = (
        lax.all_gather(query.astype(jnp.float32), "col", axis=0, tiled=True).astype(query.dtype),
        lax.all_gather(out_grad.astype(jnp.float32), "col", axis=0, tiled=True).astype(
            out_grad.dtype
        ),
        lax.all_gather(lse, "col", axis=0, tiled=True),
        lax.all_gather(delta, "col", axis=0, tiled=True),
    )
    k_all, v_all = (
        lax.all_gather(key, "row", axis=0, tiled=True),
        lax.all_gather(value, "row", axis=0, tiled=True),
    )
    q_pos = local_positions(positions, "col")
    k_pos = local_positions(positions, "row")
    q_grads, key_acc, value_acc = gradients(
        q_all, do_all, k_all, v_all, q_pos, k_pos, lse_all, delta_all
    )
    query_grad = lax.psum_scatter(q_grads, "col", scatter_dimension=0, tiled=True)
    key_grad, value_grad = (
        lax.psum_scatter(key_acc, "row", scatter_dimension=0, tiled=True),
        lax.psum_scatter(value_acc, "row", scatter_dimension=0, tiled=True),
    )
    return (
        query_grad.astype(jnp.bfloat16),
        key_grad.astype(jnp.bfloat16),
        value_grad.astype(jnp.bfloat16),
    )


def solution(mesh):
    return jax.shard_map(
        body,
        mesh=mesh,
        in_specs=(
            P(("row", "col"), None),
            P(("row", "col"), None),
            P(("row", "col"), None),
            P(("row", "col"), None),
            P(("row", "col"), None),
            P(("row", "col"), None),
            P(),
        ),
        out_specs=(P(("row", "col"), None), P(("row", "col"), None), P(("row", "col"), None)),
        check_vma=False,
    )
```

profile of v0, /device:TPU:1, one launch (start us, length us, event | category | flops | bytes accessed | tf_op | source)
XLA Modules:
  0.0 592.9 jit_solution(8166763326999523585)
XLA Ops:
  10.0 60.6 %all_gather.21 = f32[4096,2]{1,0:T(8,128)S(1)} all-gather(f32[128,2]{1,0:T(8,128)S(1)} %reduce_sum.9), channel_id=1, replica_groups=mesh['row'=8,'col'=32] {'col'}, dimensions={0}, use_global_device_ids=true | all-gather | bytes 33792 | tf_op jit(solution)/shard_map/all_gather | solution.py:106
  71.2 37.9 %all_gather.19 = f32[4096,2]{0,1:T(2,128)S(1)} all-gather(f32[128,2]{0,1:T(2,128)S(1)} %copy-done.4), channel_id=1, replica_groups=mesh['row'=8,'col'=32] {'col'}, dimensions={0}, use_global_device_ids=true | all-gather | bytes 33792 | tf_op jit(solution)/shard_map/all_gather | solution.py:105
  109.2 39.3 %all_gather.22 = bf16[1024,128]{1,0:T(8,128)(2,1)S(1)} all-gather(bf16[128,128]{1,0:T(8,128)(2,1)S(1)} %copy-done.2), channel_id=1, replica_groups=mesh['row'=8,'col'=32] {'row'}, dimensions={0}, use_global_device_ids=true | all-gather | bytes 294912 | tf_op jit(solution)/shard_map/all_gather | solution.py:109
  148.5 38.7 %all_gather.23 = bf16[1024,128]{1,0:T(8,128)(2,1)S(1)} all-gather(bf16[128,128]{1,0:T(8,128)(2,1)S(1)} %copy-done.3), channel_id=1, replica_groups=mesh['row'=8,'col'=32] {'row'}, dimensions={0}, use_global_device_ids=true | all-gather | bytes 294912 | tf_op jit(solution)/shard_map/all_gather | solution.py:110
  187.2 4.0 reshape.120
  191.2 4.0 reshape.121
  195.2 65.2 %while.31 = (s32[]{:T(128)}, f32[2,512,1,128]{3,1,2,0:T(8,128)S(1)}, f32[2,512,1,128]{3,1,2,0:T(8,128)S(1)}, f32[8,512,1,2,128]{4,3,1,0,2:T(2,128)}, s32[8,512]{...) while((s32[]{:T(128)}, ...), condition=%wide.region_4.5_spmd, body=%wide.region_1.4_spmd.sunk | while | flops 675545088 | bytes 19837404 | solution.py:91
  196.8 5.5 while.32
  204.9 5.5 while.32
  211.6 1.4 constant_dynamic-slice_fusion.14
  213.1 5.5 while.32
  221.2 5.5 while.32
  227.9 1.4 constant_dynamic-slice_fusion.14
  229.4 5.5 while.32
  237.5 5.5 while.32
  245.7 5.5 while.32
  253.8 5.5 while.32
  262.4 4.4 copy.51
  266.8 84.5 %reduce-scatter.8.cloned.1.call-done = f32[128,128]{1,0:T(8,128)} async-done(((f32[1024,128]{1,0:T(8,128)}), f32[128,128]{1,0:T(8,128)}) %reduce-scatter.8.cloned.1.call-update) | async-done | bytes 65552 | tf_op jit(solution)/shard_map/reduce_scatter | solution.py:120
  351.3 1.5 convert_element_type.38
  352.8 83.2 %reduce-scatter.6.cloned.1.call-done = f32[128,128]{1,0:T(8,128)} async-done(((f32[1024,128]{1,0:T(8,128)}), f32[128,128]{1,0:T(8,128)}) %reduce-scatter.6.cloned.1.call-update) | async-done | bytes 65552 | tf_op jit(solution)/shard_map/reduce_scatter | solution.py:119
  436.0 1.5 convert_element_type.37
  437.4 147.4 %reduce-scatter.4.cloned.1.call-done = f32[128,256]{1,0:T(8,128)} async-done(((f32[4096,256]{1,0:T(8,128)}), f32[128,256]{1,0:T(8,128)}) %reduce-scatter.4.cloned.1.call-update) | async-done | bytes 131088 | tf_op jit(solution)/shard_map/reduce_scatter | solution.py:117
  584.8 1.5 convert_element_type.36
  (240 shorter events, 66.1 us)
Async XLA Ops:
  7.2 1.6 copy-start
  7.2 180.0 %all-gather.3.cloned.1.call-start = ((), (), s32[]{:S(2)}) async-start(), calls=%async_computation.3 | async-start | bytes 2162688 | tf_op jit(solution)/shard_map/all_gather | solution.py:101
  7.9 183.3 %all-gather.5.cloned.1.call-start = ((), (), s32[]{:S(2)}) async-start(), calls=%async_computation.4 | async-start | bytes 2162688 | tf_op jit(solution)/shard_map/all_gather | solution.py:102
  8.7 342.6 %reduce-scatter.8.cloned.1.call-start = ((), (), s32[]{:S(2)}) async-start(), calls=%async_computation.7 | async-start | bytes 589824 | tf_op jit(solution)/shard_map/reduce_scatter | solution.py:120
  10.0 61.2 %copy-start.4 = (f32[128,2]{0,1:T(2,128)S(1)}, f32[128,2]{0,1:T(2,128)}, u32[]{:S(2)}) copy-start(f32[128,2]{0,1:T(2,128)} %param.16) | copy-start | bytes 3076
  10.0 99.2 %copy-start.2 = (bf16[128,128]{1,0:T(8,128)(2,1)S(1)}, bf16[128,128]{1,0:T(8,128)(2,1)}, u32[]{:S(2)}) copy-start(bf16[128,128]{1,0:T(8,128)(2,1)} %param.12) | copy-start | bytes 98308
  10.0 138.5 %copy-start.3 = (bf16[128,128]{1,0:T(8,128)(2,1)S(1)}, bf16[128,128]{1,0:T(8,128)(2,1)}, u32[]{:S(2)}) copy-start(bf16[128,128]{1,0:T(8,128)(2,1)} %param.13) | copy-start | bytes 98308
  260.5 0.8 copy-start.1
  261.3 174.6 %reduce-scatter.6.cloned.1.call-start = ((), (), s32[]{:S(2)}) async-start(), calls=%async_computation.6 | async-start | bytes 589824 | tf_op jit(solution)/shard_map/reduce_scatter | solution.py:119
  262.3 322.5 %reduce-scatter.4.cloned.1.call-start = ((), (), s32[]{:S(2)}) async-start(), calls=%async_computation.5 | async-start | bytes 4325376 | tf_op jit(solution)/shard_map/reduce_scatter | solution.py:117
Sparse Core Ops, SparseCore 0:
  9.9 66.6 all-gather.2
  78.4 59.1 all-gather.4
  261.5 89.8 reduce-scatter.7
  355.5 80.3 reduce-scatter.5
  438.3 146.4 reduce-scatter.3
where the time goes:
time: 597 us; the launch traced here: 593 us
  waiting for transfers between devices  317 us (53%)
  blocking collectives  177 us (30%)
  matrix products  38.3 us (6%)
  local copies, waits for them, and re-layouts  35.5 us (6%)
  between operations  13.9 us (2%)
  other arithmetic  10.3 us (2%)
    reduce_scatter x1, waiting for transfers between devices, body(): lax.psum_scatter(q_grads, 'col', scatter_dimension=0, tiled=True)  147 us
    reduce_scatter x1, waiting for transfers between devices, body(): lax.psum_scatter(value_acc, 'row', scatter_dimension=0, tiled=True)  84.5 us
    reduce_scatter x1, waiting for transfers between devices, body(): lax.psum_scatter(key_acc, 'row', scatter_dimension=0, tiled=True)  83.2 us
    all_gather x1, blocking collectives, body(): lax.all_gather(delta, 'col', axis=0, tiled=True)  60.6 us
    all_gather x1, blocking collectives, body(): lax.all_gather(key, 'row', axis=0, tiled=True)  39.3 us
    all_gather x1, blocking collectives, body(): lax.all_gather(value, 'row', axis=0, tiled=True)  38.7 us
    all_gather x1, blocking collectives, body(): lax.all_gather(lse, 'col', axis=0, tiled=True)  37.9 us
  transfers between devices with their start and end apart: 5, of which 3 were waited for; matrix products, arithmetic and copies ran while one was open for 2% of the time, Pallas kernels for 0%

commit v1 on v0

v1 whole, which is shorter than its diff:
```python
import functools
import math

import jax
import jax.numpy as jnp
from jax import lax
from jax.experimental import pallas as pl
from jax.experimental.pallas import tpu as pltpu
from jax.sharding import PartitionSpec as P

F32 = jnp.float32
BF16 = jnp.bfloat16
MESH = pl.DeviceIdType.MESH
ROWS = 128
DIM = 128
NX, NY, NZ = 4, 4, 8
AUG = 16
REST = 112
SCALE = 1.0 / math.sqrt(DIM)
EXP_SCALE = math.log2(math.e) / math.sqrt(DIM)
FAR = -1e30
NT = (((1,), (1,)), ((), ()))

TILES = (
    (0, 0), (0, 1), (0, 3), (3, 1), (3, 3), (1, 1), (1, 3), (2, 1),
    (2, 3), (2, 2), (2, 0), (1, 2), (1, 0), (0, 2), (3, 2), (3, 0),
)


def table(values):
    total = 0
    for at, value in enumerate(values):
        total += value * 4**at
    return total


def place():
    row, col = lax.axis_index("row"), lax.axis_index("col")
    x, z_lo, core = col // 8, (col // 2) % 4, col % 2
    y, z_hi = row // 2, row % 2
    return x, y, z_hi * 4 + z_lo, core


def device(x, y, z, core):
    return (y * 2 + z // 4, x * 8 + (z % 4) * 2 + core)


def kernel(
    query, key, value, out_grad, attn_out, lse, positions,
    query_grad, key_grad, value_grad,
    qd, qm, kv, kt, ka, kp, dq, dk, dv,
    sib_out, sib_in, dq_out, dq_in, dkv_out, dkv_in,
    kv_send, kv_recv, ring_send, q_recv, pair_send,
    sib_send, sib_recv, dq_send, dq_recv, dkv_send, dkv_recv,
):
    x, y, z, core = place()
    other = 1 - core

    def plane(ox, oy):
        return device((x + ox) % NX, (y + oy) % NY, z, core)

    def along(oz, which=None):
        return device(x, y, (z + oz) % NZ, core if which is None else which)

    sibling = device(x, y, z, other)
    plane_offsets = [(ox, oy) for oy in (0, 1, 3, 2) for ox in (1, 3, 2, 0) if ox or oy]

    barrier = pltpu.get_barrier_semaphore()
    peers = [plane(ox, oy) for ox, oy in plane_offsets]
    peers += [along(oz) for oz in range(1, NZ)] + [sibling]
    for peer in peers:
        pl.semaphore_signal(barrier, inc=1, device_id=peer, device_id_type=MESH)

    kv[0, 0] = key[...]
    kv[0, 1] = value[...]
    line = lax.broadcasted_iota(jnp.int32, (AUG, ROWS), 0)

    def split_rows(term):
        high = term.astype(BF16).astype(F32)
        rest = term - high
        middle = rest.astype(BF16).astype(F32)
        low = rest - middle
        picked = jnp.where(line == 0, high, jnp.where(line == 1, middle, low))
        return jnp.where(line < 3, picked, 0.0).astype(BF16)

    for head in range(2):
        cut = pl.ds(head * DIM, DIM)
        grads, outs = out_grad[:, cut], attn_out[:, cut]
        delta = jnp.sum((grads.astype(F32) * outs.astype(F32)).T, axis=0, keepdims=True)
        wide = jnp.broadcast_to(lse[:, head : head + 1], (ROWS, ROWS)).T
        qd[0, head, 0:DIM] = query[:, cut].T
        qd[0, head, DIM : DIM + AUG] = split_rows(wide[0:1] * -math.sqrt(DIM))
        qd[0, 2 + head, 0:DIM] = grads.T
        qd[0, 2 + head, DIM : DIM + AUG] = split_rows(-delta)

    pl.semaphore_wait(barrier, len(peers))

    def ring_copy(source, target, part, at, oz):
        return pltpu.make_async_remote_copy(
            src_ref=qd.at[source] if part is None else qd.at[source, pl.ds(part * 2, 2)],
            dst_ref=qd.at[target] if part is None else qd.at[target, pl.ds(part * 2, 2)],
            send_sem=ring_send.at[at],
            recv_sem=q_recv.at[16 if part else target],
            device_id=along(oz),
            device_id_type=MESH,
        )

    def pair_copy(oz):
        return pltpu.make_async_remote_copy(
            src_ref=qd.at[2 * oz],
            dst_ref=qd.at[2 * oz + 1],
            send_sem=pair_send.at[oz],
            recv_sem=q_recv.at[2 * oz + 1],
            device_id=sibling,
            device_id_type=MESH,
        )

    rights = [ring_copy(0, 14, None, 0, 1), ring_copy(14, 12, None, 1, 1),
              ring_copy(12, 10, None, 2, 1), ring_copy(10, 8, 0, 3, 1)]
    lefts = [ring_copy(0, 2, None, 4, -1 + NZ), ring_copy(2, 4, None, 5, -1 + NZ),
             ring_copy(4, 6, None, 6, -1 + NZ), ring_copy(6, 8, 1, 7, -1 + NZ)]
    pairs = [pair_copy(oz) for oz in range(NZ)]

    def kv_copy(ox, oy):
        there = (NY - oy) % NY * 4 + (NX - ox) % NX
        return pltpu.make_async_remote_copy(
            src_ref=kv.at[0],
            dst_ref=kv.at[there],
            send_sem=kv_send.at[oy * 4 + ox],
            recv_sem=kv_recv.at[there],
            device_id=plane(ox, oy),
            device_id_type=MESH,
        )

    kv_copies = {offset: kv_copy(*offset) for offset in plane_offsets}

    rights[0].start()
    lefts[0].start()
    for offset in plane_offsets:
        kv_copies[offset].start()
    pairs[0].start()

    dq[...] = jnp.zeros_like(dq)
    dk[...] = jnp.zeros_like(dk)
    dv[...] = jnp.zeros_like(dv)
    lane = lax.broadcasted_iota(jnp.int32, (ROWS, ROWS), 1)
    block = lax.broadcasted_iota(jnp.int32, (ROWS, ROWS), 0) // 64
    for slot in range(16):
        hot = (lane < 3) | (lane == AUG + 2 * slot + block)
        ka[slot] = jnp.where(hot, 1.0, 0.0).astype(BF16)
        r, c = plane(slot % 4, slot // 4)
        places = positions[pl.ds(r * 32 + c, 1), :] // 64
        kp[2 * slot : 2 * slot + 1, :] = jnp.broadcast_to(places[:, 0:1], (1, ROWS))
        kp[2 * slot + 1 : 2 * slot + 2, :] = jnp.broadcast_to(places[:, 64:65], (1, ROWS))
    for slot in range(16):
        r, c = along(slot // 2, other if slot % 2 else core)
        places = positions[pl.ds(r * 32 + c, 1), :] // 64
        bias = jnp.where(kp[...] < places, 0.0, FAR)
        qm[slot] = jnp.concatenate([bias, jnp.zeros((REST - 32, ROWS), F32)], 0).astype(BF16)

    none = jnp.zeros((REST, ROWS), BF16)

    def turn(slot):
        kt[slot] = kv[slot, 0].T

    turn(0)
    keys = jnp.concatenate([kv[0, 0], ka[0]], 1)
    values = jnp.concatenate([kv[0, 1], ka[0]], 1)
    q_own = [qd[0, head] for head in range(4)]
    q_cat = jnp.concatenate([jnp.concatenate([part, none], 0) for part in q_own[:2]], 1)
    d_cat = jnp.concatenate([jnp.concatenate([part, none], 0) for part in q_own[2:]], 1)
    scores = jnp.dot(keys, q_cat, preferred_element_type=F32)
    dprobs = jnp.dot(values, d_cat, preferred_element_type=F32)
    at_key = lax.broadcasted_iota(jnp.int32, (ROWS, 2 * ROWS), 0)
    at_row = lax.broadcasted_iota(jnp.int32, (ROWS, 2 * ROWS), 1) % ROWS
    inside = (at_key <= at_row) & (at_key // 64 == at_row // 64)
    probs = jnp.where(inside, jnp.exp2(scores * EXP_SCALE), 0.0)
    dscores = (probs * dprobs).astype(BF16)
    dv[0] = lax.dot_general(d_cat[:DIM], probs.astype(BF16), NT, preferred_element_type=F32)
    dk[0] = lax.dot_general(q_cat[:DIM], dscores, NT, preferred_element_type=F32)
    part = jnp.dot(kt[0], dscores, preferred_element_type=F32)
    dq[0] = jnp.concatenate([part[:, :ROWS], part[:, ROWS:]], 0)

    def wait_keys(group):
        for ox in range(NX):
            if ox or group:
                offset = ((NX - ox) % NX, (NY - group) % NY)
                kv_copies[offset].wait_recv()
                turn(group * 4 + ox)

    def dkv_copy(ox, oy):
        there = (NY - oy) % NY * 4 + (NX - ox) % NX
        return pltpu.make_async_remote_copy(
            src_ref=dkv_out.at[oy * 4 + ox],
            dst_ref=dkv_in.at[there],
            send_sem=dkv_send.at[oy * 4 + ox],
            recv_sem=dkv_recv.at[there],
            device_id=plane(ox, oy),
            device_id_type=MESH,
        )

    dkv_copies = {offset: dkv_copy(*offset) for offset in plane_offsets}

    def send_keys(group):
        for ox in (2, 1, 3, 0):
            if ox or group:
                slot = group * 4 + ox
                dkv_out[slot, 0:DIM] = dk[slot].astype(BF16)
                dkv_out[slot, DIM:] = dv[slot].astype(BF16)
                dkv_copies[(ox, group)].start()

    def sib_copy(oz):
        return pltpu.make_async_remote_copy(
            src_ref=sib_out.at[oz],
            dst_ref=sib_in.at[oz],
            send_sem=sib_send.at[oz],
            recv_sem=sib_recv.at[oz],
            device_id=sibling,
            device_id_type=MESH,
        )

    sib_copies = [sib_copy(oz) for oz in range(NZ)]

    def dq_copy(oz):
        return pltpu.make_async_remote_copy(
            src_ref=dq_out.at[oz],
            dst_ref=dq_in.at[NZ - oz],
            send_sem=dq_send.at[oz],
            recv_sem=dq_recv.at[NZ - oz],
            device_id=along(oz),
            device_id_type=MESH,
        )

    dq_copies = {oz: dq_copy(oz) for oz in range(1, NZ)}

    def swap_queries(group):
        for oz in (2 * group, 2 * group + 1):
            sib_out[oz] = dq[2 * oz + 1].astype(BF16)
            sib_copies[oz].start()

    def send_queries(group):
        for oz in (2 * group, 2 * group + 1):
            sib_copies[oz].wait_recv()
            total = dq[2 * oz] + sib_in[oz].astype(F32)
            if oz:
                dq_out[oz] = total.astype(BF16)
                dq_copies[oz].start()
            else:
                dq[0] = total

    def hop(step):
        rights[step - 1].wait_recv()
        rights[step].start()
        lefts[step - 1].wait_recv()
        lefts[step].start()
        pairs[NZ - step].start()
        pairs[step].start()

    def before(step):
        if step == 0:
            hop(1)
            wait_keys(0)
            pairs[0].wait_recv()
            pairs[1].wait_recv()
        if step == 1:
            wait_keys(1)
        if step == 2:
            hop(2)
            wait_keys(3)
        if step == 3:
            pairs[7].wait_recv()
            pairs[6].wait_recv()
        if step == 4:
            hop(3)
        if step == 5:
            pairs[2].wait_recv()
            pairs[3].wait_recv()
            wait_keys(2)
        if step == 6:
            rights[3].wait_recv()
            lefts[3].wait_recv()
            pairs[4].start()
        if step == 7:
            pairs[4].wait_recv()
            pairs[5].wait_recv()

    def after(step):
        if step == 7:
            send_keys(1)
        if step == 8:
            send_keys(3)
        if step == 10:
            swap_queries(2)
        if step == 11:
            send_queries(2)
        if step == 12:
            swap_queries(1)
        if step == 13:
            send_queries(1)
            swap_queries(0)
        if step == 14:
            send_keys(2)
            send_queries(0)
        if step == 15:
            swap_queries(3)
            send_keys(0)
            send_queries(3)

    def tile(at_q, at_k):
        first_q, first_k = at_q * 4, at_k * 4
        marks = ka[pl.ds(first_k, 4)].reshape(4 * ROWS, ROWS)
        k_part = kv[pl.ds(first_k, 4), 0].reshape(4 * ROWS, DIM)
        v_part = kv[pl.ds(first_k, 4), 1].reshape(4 * ROWS, DIM)
        k_wide = jnp.concatenate([k_part, marks], 1)
        v_wide = jnp.concatenate([v_part, marks], 1)
        q_cols = [
            jnp.concatenate([qd[first_q + a, head], qm[first_q + a]], 0)
            for a in range(4)
            for head in range(2)
        ]
        d_cols = [
            jnp.concatenate([qd[first_q + a, 2 + head], none], 0)
            for a in range(4)
            for head in range(2)
        ]
        q_wide = jnp.concatenate(q_cols, 1)
        d_wide = jnp.concatenate(d_cols, 1)
        scores = jnp.dot(k_wide, q_wide, preferred_element_type=F32)
        dprobs = jnp.dot(v_wide, d_wide, preferred_element_type=F32)
        probs = jnp.exp2(scores * EXP_SCALE)
        dscores = (probs * dprobs).astype(BF16)
        v_sum = lax.dot_general(
            d_wide[:DIM], probs.astype(BF16), NT, preferred_element_type=F32
        )
        k_sum = lax.dot_general(q_wide[:DIM], dscores, NT, preferred_element_type=F32)
        k_turned = jnp.concatenate([kt[first_k + a] for a in range(4)], 1)
        q_sum = jnp.dot(k_turned, dscores, preferred_element_type=F32)
        for a in range(4):
            dv[first_k + a] += v_sum[:, a * ROWS : (a + 1) * ROWS]
            dk[first_k + a] += k_sum[:, a * ROWS : (a + 1) * ROWS]
            for head in range(2):
                col = (2 * a + head) * ROWS
                dq[first_q + a, pl.ds(head * DIM, DIM)] += q_sum[:, col : col + ROWS]

    q_tables = [table(q for q, _ in TILES[8 * half : 8 * half + 8]) for half in range(2)]
    k_tables = [table(k for _, k in TILES[8 * half : 8 * half + 8]) for half in range(2)]

    def run_half(half, carry):
        q_list = q_tables[0] + half * (q_tables[1] - q_tables[0])
        k_list = k_tables[0] + half * (k_tables[1] - k_tables[0])

        def run_tile(at, lists):
            q_list, k_list = lists
            step = half * 8 + at
            for n in range(16):
                pl.when(step == n)(functools.partial(before, n))
            tile(q_list % 4, k_list % 4)
            for n in range(16):
                pl.when(step == n)(functools.partial(after, n))
            return q_list // 4, k_list // 4

        lax.fori_loop(0, 8, run_tile, (q_list, k_list))
        return carry

    lax.fori_loop(0, 2, run_half, 0)

    for oz in range(1, NZ):
        dq_copies[oz].wait_recv()
    total = dq[0]
    for oz in range(1, NZ):
        total = total + dq_in[oz].astype(F32)
    total = total * SCALE
    for head in range(2):
        part = total[head * DIM : (head + 1) * DIM]
        query_grad[:, pl.ds(head * DIM, DIM)] = part.T.astype(BF16)
    for offset in plane_offsets:
        dkv_copies[offset].wait_recv()
    k_total, v_total = dk[0], dv[0]
    for slot in range(1, 16):
        k_total = k_total + dkv_in[slot, 0:DIM].astype(F32)
        v_total = v_total + dkv_in[slot, DIM:].astype(F32)
    key_grad[...] = (k_total * SCALE).T.astype(BF16)
    value_grad[...] = v_total.T.astype(BF16)

    for copies in (kv_copies, dkv_copies, dq_copies):
        for copy in copies.values():
            copy.wait_send()
    for copy in rights + lefts + pairs + sib_copies:
        copy.wait_send()


def body(query, key, value, out_grad, attn_out, lse, positions):
    vmem = pl.BlockSpec(memory_space=pltpu.VMEM)
    dma = pltpu.SemaphoreType.DMA
    return pl.pallas_call(
        kernel,
        out_shape=(
            jax.ShapeDtypeStruct((ROWS, 2 * DIM), BF16),
            jax.ShapeDtypeStruct((ROWS, DIM), BF16),
            jax.ShapeDtypeStruct((ROWS, DIM), BF16),
        ),
        in_specs=[vmem] * 7,
        out_specs=[vmem] * 3,
        scratch_shapes=[
            pltpu.VMEM((16, 4, DIM + AUG, ROWS), BF16),
            pltpu.VMEM((16, REST, ROWS), BF16),
            pltpu.VMEM((16, 2, ROWS, DIM), BF16),
            pltpu.VMEM((16, DIM, ROWS), BF16),
            pltpu.VMEM((16, ROWS, ROWS), BF16),
            pltpu.VMEM((32, ROWS), jnp.int32),
            pltpu.VMEM((16, 2 * DIM, ROWS), F32),
            pltpu.VMEM((16, DIM, ROWS), F32),
            pltpu.VMEM((16, DIM, ROWS), F32),
            pltpu.VMEM((8, 2 * DIM, ROWS), BF16),
            pltpu.VMEM((8, 2 * DIM, ROWS), BF16),
            pltpu.VMEM((8, 2 * DIM, ROWS), BF16),
            pltpu.VMEM((8, 2 * DIM, ROWS), BF16),
            pltpu.VMEM((16, 2 * DIM, ROWS), BF16),
            pltpu.VMEM((16, 2 * DIM, ROWS), BF16),
            dma((16,)),
            dma((16,)),
            dma((8,)),
            dma((17,)),
            dma((8,)),
            dma((8,)),
            dma((8,)),
            dma((8,)),
            dma((8,)),
            dma((16,)),
            dma((16,)),
        ],
        compiler_params=pltpu.CompilerParams(
            collective_id=0, has_side_effects=True, vmem_limit_bytes=56 * 2**20
        ),
    )(query, key, value, out_grad, attn_out, lse, positions.reshape(256, ROWS))


def solution(mesh):
    split = P(("row", "col"), None)
    return jax.shard_map(
        body,
        mesh=mesh,
        in_specs=(split,) * 6 + (P(),),
        out_specs=(split,) * 3,
        check_vma=False,
    )
```

time: 597 us -> 65.8 us (0.11)
  waiting for transfers between devices: 317 us -> 0 us
  blocking collectives: 177 us -> 0 us
  Pallas kernels: 0 us -> 60.7 us
  matrix products: 38.3 us -> 0 us
  local copies, waits for them, and re-layouts: 35.5 us -> 4.28 us
  between operations: 13.9 us -> 0.66 us
  other arithmetic: 10.3 us -> 0 us
    reduce_scatter x3 -> x0, waiting for transfers between devices: 315 us -> none  [the longest x1 147 us: body(): lax.psum_scatter(q_grads, 'col', scatter_dimension=0, tiled=True)]
    all_gather x4 -> x0, blocking collectives: 177 us -> none  [the longest x1 60.6 us: body(): lax.all_gather(delta, 'col', axis=0, tiled=True)]
    pallas_call x0 -> x1, Pallas kernels: none -> 60.7 us  [body(): pl.pallas_call(kernel, out_shape=(jax.ShapeDtypeStruct((ROWS, 2 * DIM), B...]
    dot_general x80 -> x0, matrix products: 38.3 us -> none  [the longest x16 11.1 us: per_key(): jnp.einsum('qgcd,kgd->gcqk', q_block, k_block, preferred_element_type=jnp...]
    dynamic_slice x74 -> x0, local copies, waits for them, and re-layouts: 12.8 us -> none  [the longest x40 11.9 us: gradients(): (key_acc, value_acc), q_grads = lax.scan(per_query, (zeros, zeros), pieces)]
    dynamic_update_slice x16 -> x0, local copies, waits for them, and re-layouts: 8.65 us -> none  [gradients(): (key_acc, value_acc), q_grads = lax.scan(per_query, (zeros, zeros), pieces)]
    another operation x6 -> x0, local copies, waits for them, and re-layouts: 8.01 us -> none  [the longest x4 7.94 us: split_blocks(): return array.reshape((array.shape[0] // size, size) + array.shape[1:])]
  transfers between devices with their start and end apart: 5 -> 0, of which waited for: 3 -> 0; matrix products, arithmetic and copies ran while one was open for 2% -> 0% of each run, Pallas kernels for 0% -> 0%
where the time goes in v1:
time: 65.8 us; the launch traced here: 65.6 us
  Pallas kernels  60.7 us (92%)
  local copies, waits for them, and re-layouts  4.28 us (7%)
  between operations  0.66 us (1%)
    pallas_call x1, Pallas kernels, body(): pl.pallas_call(kernel, out_shape=(jax.ShapeDtypeStruct((ROWS, 2 * DIM), B...  60.7 us
    unnamed x10, local copies, waits for them, and re-layouts  4.28 us

profile of v1, /device:TPU:1, one launch (start us, length us, event | category | flops | bytes accessed | tf_op | source)
XLA Modules:
  0.0 65.6 jit_solution(854633206100281397)
XLA Ops:
  0.6 0.0 copy-start.2
  0.6 0.7 %copy-done.2 = f32[128,2]{0,1:T(2,128)S(1)} copy-done((f32[128,2]{0,1:T(2,128)S(1)}, f32[128,2]{0,1:T(2,128)}, u32[]{:S(2)}) %copy-start.2) | copy-done | bytes 1048
  1.3 0.7 %copy.10.lse = f32[128,2]{1,0:T(8,128)} copy(f32[128,2]{0,1:T(2,128)S(1)} %copy-done.2) | data formatting | bytes 2048 | tf_op args[5]
  2.1 60.7 %shard_map.94 = (bf16[128,256]{1,0:T(8,128)(2,1)}, bf16[128,128]{1,0:T(8,128)(2,1)}, bf16[128,128]{1,0:T(8,128)(2,1)}) custom-call(bf16[128,256]{1,0:T(8,128)(2,1)} %query.1, bf16[128,128]{1,0:T(8,128)(2,1)} %key.1, bf16[128,128]{1,0:T(8,128)(2,1)} %value.1, bf16[128,256]{1,0:T(8,128)(2,1)} %out_grad.1, bf16[128,256]{1,0:T(8,128)(2,1)} %attn_out.1, ...), custom_call_target="tpu_custom_call" | custom-call | tf_op jit(solution)/shard_map/pallas_call | solution.py:395
  62.7 0.0 copy-start.1
  62.7 1.5 %copy.14 = bf16[128,256]{1,0:T(8,128)(2,1)} copy(bf16[128,256]{1,0:T(8,128)(2,1)} %get-tuple-element.6) | data formatting | bytes 131072
  64.2 0.0 copy-done.1
  64.2 0.0 copy-start
  64.2 0.6 copy.15
  64.8 0.2 copy-done
  65.0 0.6 copy.16
Async XLA Ops:
  0.6 0.7 %copy-start.2 = (f32[128,2]{0,1:T(2,128)S(1)}, f32[128,2]{0,1:T(2,128)}, u32[]{:S(2)}) copy-start(f32[128,2]{0,1:T(2,128)} %param.12) | copy-start | bytes 3076
  62.7 1.5 %copy-start.1 = (bf16[128,128]{1,0:T(8,128)(2,1)S(1)}, bf16[128,128]{1,0:T(8,128)(2,1)}, u32[]{:S(2)}) copy-start(bf16[128,128]{1,0:T(8,128)(2,1)} %get-tuple-element.7) | copy-start | bytes 98308
  64.2 0.8 %copy-start = (bf16[128,128]{1,0:T(8,128)(2,1)S(1)}, bf16[128,128]{1,0:T(8,128)(2,1)}, u32[]{:S(2)}) copy-start(bf16[128,128]{1,0:T(8,128)(2,1)} %get-tuple-element.8) | copy-start | bytes 98308

commit v2 on v1

--- a/solution.py
+++ b/solution.py
@@ -21,9 +21,17 @@
 FAR = -1e30
 NT = (((1,), (1,)), ((), ()))
 
+PAIRS = ((0, 4), (1, 7), (2, 6), (3, 5))
+SPOT = {oz: 2 * group + at for group, pair in enumerate(PAIRS) for at, oz in enumerate(pair)}
+
+KEY_SPOTS = (
+    (0, 0), (1, 0), (3, 0), (2, 0), (0, 1), (0, 3), (0, 2), (1, 1),
+    (3, 1), (1, 3), (2, 1), (1, 2), (3, 3), (2, 3), (3, 2), (2, 2),
+)
+
 TILES = (
-    (0, 0), (0, 1), (0, 3), (3, 1), (3, 3), (1, 1), (1, 3), (2, 1),
-    (2, 3), (2, 2), (2, 0), (1, 2), (1, 0), (0, 2), (3, 2), (3, 0),
+    (1, 0), (1, 1), (2, 0), (2, 1), (1, 2), (2, 2), (1, 3), (2, 3),
+    (3, 2), (3, 3), (0, 2), (0, 3), (3, 1), (3, 0), (0, 1), (0, 0),
 )
 
 
@@ -48,11 +56,13 @@
 def kernel(
     query, key, value, out_grad, attn_out, lse, positions,
     query_grad, key_grad, value_grad,
-    qd, qm, kv, kt, ka, kp, dq, dk, dv,
+    pos, qd, qm, kv, kt, ka, kp, dq, dk, dv,
     sib_out, sib_in, dq_out, dq_in, dkv_out, dkv_in,
-    kv_send, kv_recv, ring_send, q_recv, pair_send,
+    pos_sem, kv_send, kv_recv, ring_send, q_recv, pair_send,
     sib_send, sib_recv, dq_send, dq_recv, dkv_send, dkv_recv,
 ):
+    pos_copy = pltpu.make_async_copy(positions, pos, pos_sem)
+    pos_copy.start()
     x, y, z, core = place()
     other = 1 - core
 
@@ -63,10 +73,9 @@
         return device(x, y, (z + oz) % NZ, core if which is None else which)
 
     sibling = device(x, y, z, other)
-    plane_offsets = [(ox, oy) for oy in (0, 1, 3, 2) for ox in (1, 3, 2, 0) if ox or oy]
 
     barrier = pltpu.get_barrier_semaphore()
-    peers = [plane(ox, oy) for ox, oy in plane_offsets]
+    peers = [plane(ox, oy) for ox, oy in KEY_SPOTS[1:]]
     peers += [along(oz) for oz in range(1, NZ)] + [sibling]
     for peer in peers:
         pl.semaphore_signal(barrier, inc=1, device_id=peer, device_id_type=MESH)
@@ -87,58 +96,75 @@
         cut = pl.ds(head * DIM, DIM)
         grads, outs = out_grad[:, cut], attn_out[:, cut]
         delta = jnp.sum((grads.astype(F32) * outs.astype(F32)).T, axis=0, keepdims=True)
-        wide = jnp.broadcast_to(lse[:, head : head + 1], (ROWS, ROWS)).T
         qd[0, head, 0:DIM] = query[:, cut].T
-        qd[0, head, DIM : DIM + AUG] = split_rows(wide[0:1] * -math.sqrt(DIM))
+        qd[0, head, DIM : DIM + AUG] = split_rows(lse[head : head + 1, :] * -math.sqrt(DIM))
         qd[0, 2 + head, 0:DIM] = grads.T
         qd[0, 2 + head, DIM : DIM + AUG] = split_rows(-delta)
 
     pl.semaphore_wait(barrier, len(peers))
 
-    def ring_copy(source, target, part, at, oz):
-        return pltpu.make_async_remote_copy(
-            src_ref=qd.at[source] if part is None else qd.at[source, pl.ds(part * 2, 2)],
-            dst_ref=qd.at[target] if part is None else qd.at[target, pl.ds(part * 2, 2)],
-            send_sem=ring_send.at[at],
-            recv_sem=q_recv.at[16 if part else target],
-            device_id=along(oz),
-            device_id_type=MESH,
-        )
-
-    def pair_copy(oz):
-        return pltpu.make_async_remote_copy(
-            src_ref=qd.at[2 * oz],
-            dst_ref=qd.at[2 * oz + 1],
-            send_sem=pair_send.at[oz],
-            recv_sem=q_recv.at[2 * oz + 1],
+    def own_slot(oz):
+        return 2 * SPOT[oz % NZ]
+
+    def ring_copy(hop, chunk, way):
+        source, target = own_slot(way * (1 - hop)), own_slot(-way * hop)
+        cut = pl.ds(2 * chunk, 2)
+        return pltpu.make_async_remote_copy(
+            src_ref=qd.at[source, cut],
+            dst_ref=qd.at[target, cut],
+            send_sem=ring_send.at[0 if way > 0 else 1, hop - 1, chunk],
+            recv_sem=q_recv.at[target, chunk],
+            device_id=along(way % NZ),
+            device_id_type=MESH,
+        )
+
+    def pair_copy(oz, chunk):
+        slot = own_slot(oz)
+        cut = pl.ds(2 * chunk, 2)
+        return pltpu.make_async_remote_copy(
+            src_ref=qd.at[slot, cut],
+            dst_ref=qd.at[slot + 1, cut],
+            send_sem=pair_send.at[oz, chunk],
+            recv_sem=q_recv.at[slot + 1, chunk],
             device_id=sibling,
             device_id_type=MESH,
         )
 
-    rights = [ring_copy(0, 14, None, 0, 1), ring_copy(14, 12, None, 1, 1),
-              ring_copy(12, 10, None, 2, 1), ring_copy(10, 8, 0, 3, 1)]
-    lefts = [ring_copy(0, 2, None, 4, -1 + NZ), ring_copy(2, 4, None, 5, -1 + NZ),
-             ring_copy(4, 6, None, 6, -1 + NZ), ring_copy(6, 8, 1, 7, -1 + NZ)]
-    pairs = [pair_copy(oz) for oz in range(NZ)]
-
-    def kv_copy(ox, oy):
-        there = (NY - oy) % NY * 4 + (NX - ox) % NX
+    ring = {
+        (hop, chunk, way): ring_copy(hop, chunk, way)
+        for hop in range(1, 5)
+        for chunk in range(2)
+        for way in (1, -1)
+        if hop < 4 or (way > 0) == (chunk == 0)
+    }
+    pairs = {(oz, chunk): pair_copy(oz, chunk) for oz in range(NZ) for chunk in range(2)}
+
+    def kv_copy(slot):
+        ox, oy = KEY_SPOTS[slot]
         return pltpu.make_async_remote_copy(
             src_ref=kv.at[0],
-            dst_ref=kv.at[there],
-            send_sem=kv_send.at[oy * 4 + ox],
-            recv_sem=kv_recv.at[there],
-            device_id=plane(ox, oy),
-            device_id_type=MESH,
-        )
-
-    kv_copies = {offset: kv_copy(*offset) for offset in plane_offsets}
-
-    rights[0].start()
-    lefts[0].start()
-    for offset in plane_offsets:
-        kv_copies[offset].start()
-    pairs[0].start()
+            dst_ref=kv.at[slot],
+            send_sem=kv_send.at[slot],
+            recv_sem=kv_recv.at[slot],
+            device_id=plane(NX - ox, NY - oy),
+            device_id_type=MESH,
+        )
+
+    kv_copies = {slot: kv_copy(slot) for slot in range(1, 16)}
+
+    def share_keys(group):
+        for slot in range(4 * group, 4 * group + 4):
+            if slot:
+                kv_copies[slot].start()
+
+    for chunk in range(2):
+        for way in (1, -1):
+            ring[(1, chunk, way)].start()
+    share_keys(0)
+    share_keys(1)
+    for chunk in range(2):
+        pairs[(0, chunk)].start()
+    pos_copy.wait()
 
     dq[...] = jnp.zeros_like(dq)
     dk[...] = jnp.zeros_like(dk)
@@ -148,13 +174,13 @@
     for slot in range(16):
         hot = (lane < 3) | (lane == AUG + 2 * slot + block)
         ka[slot] = jnp.where(hot, 1.0, 0.0).astype(BF16)
-        r, c = plane(slot % 4, slot // 4)
-        places = positions[pl.ds(r * 32 + c, 1), :] // 64
+        r, c = plane(*KEY_SPOTS[slot])
+        places = pos[pl.ds(r * 32 + c, 1), :] // 64
         kp[2 * slot : 2 * slot + 1, :] = jnp.broadcast_to(places[:, 0:1], (1, ROWS))
         kp[2 * slot + 1 : 2 * slot + 2, :] = jnp.broadcast_to(places[:, 64:65], (1, ROWS))
     for slot in range(16):
-        r, c = along(slot // 2, other if slot % 2 else core)
-        places = positions[pl.ds(r * 32 + c, 1), :] // 64
+        r, c = along(PAIRS[slot // 4][slot // 2 % 2], other if slot % 2 else core)
+        places = pos[pl.ds(r * 32 + c, 1), :] // 64
         bias = jnp.where(kp[...] < places, 0.0, FAR)
         qm[slot] = jnp.concatenate([bias, jnp.zeros((REST - 32, ROWS), F32)], 0).astype(BF16)
 
@@ -182,32 +208,29 @@
     dq[0] = jnp.concatenate([part[:, :ROWS], part[:, ROWS:]], 0)
 
     def wait_keys(group):
-        for ox in range(NX):
-            if ox or group:
-                offset = ((NX - ox) % NX, (NY - group) % NY)
-                kv_copies[offset].wait_recv()
-                turn(group * 4 + ox)
-
-    def dkv_copy(ox, oy):
-        there = (NY - oy) % NY * 4 + (NX - ox) % NX
-        return pltpu.make_async_remote_copy(
-            src_ref=dkv_out.at[oy * 4 + ox],
-            dst_ref=dkv_in.at[there],
-            send_sem=dkv_send.at[oy * 4 + ox],
-            recv_sem=dkv_recv.at[there],
-            device_id=plane(ox, oy),
-            device_id_type=MESH,
-        )
-
-    dkv_copies = {offset: dkv_copy(*offset) for offset in plane_offsets}
+        for slot in range(4 * group, 4 * group + 4):
+            if slot:
+                kv_copies[slot].wait_recv()
+                turn(slot)
+
+    def dkv_copy(slot):
+        return pltpu.make_async_remote_copy(
+            src_ref=dkv_out.at[slot],
+            dst_ref=dkv_in.at[slot],
+            send_sem=dkv_send.at[slot],
+            recv_sem=dkv_recv.at[slot],
+            device_id=plane(*KEY_SPOTS[slot]),
+            device_id_type=MESH,
+        )
+
+    dkv_copies = {slot: dkv_copy(slot) for slot in range(1, 16)}
 
     def send_keys(group):
-        for ox in (2, 1, 3, 0):
-            if ox or group:
-                slot = group * 4 + ox
+        for slot in range(4 * group + 3, 4 * group - 1, -1):
+            if slot:
                 dkv_out[slot, 0:DIM] = dk[slot].astype(BF16)
                 dkv_out[slot, DIM:] = dv[slot].astype(BF16)
-                dkv_copies[(ox, group)].start()
+                dkv_copies[slot].start()
 
     def sib_copy(oz):
         return pltpu.make_async_remote_copy(
@@ -234,77 +257,83 @@
     dq_copies = {oz: dq_copy(oz) for oz in range(1, NZ)}
 
     def swap_queries(group):
-        for oz in (2 * group, 2 * group + 1):
-            sib_out[oz] = dq[2 * oz + 1].astype(BF16)
+        for oz in PAIRS[group]:
+            sib_out[oz] = dq[own_slot(oz) + 1].astype(BF16)
             sib_copies[oz].start()
 
     def send_queries(group):
-        for oz in (2 * group, 2 * group + 1):
+        for oz in PAIRS[group]:
             sib_copies[oz].wait_recv()
-            total = dq[2 * oz] + sib_in[oz].astype(F32)
+            total = dq[own_slot(oz)] + sib_in[oz].astype(F32)
             if oz:
                 dq_out[oz] = total.astype(BF16)
                 dq_copies[oz].start()
             else:
                 dq[0] = total
 
-    def hop(step):
-        rights[step - 1].wait_recv()
-        rights[step].start()
-        lefts[step - 1].wait_recv()
-        lefts[step].start()
-        pairs[NZ - step].start()
-        pairs[step].start()
+    def relay(hop, chunk):
+        for way in (1, -1):
+            if (hop, chunk, way) in ring:
+                ring[(hop, chunk, way)].wait_recv()
+                if (hop + 1, chunk, way) in ring:
+                    ring[(hop + 1, chunk, way)].start()
+                pairs[(-way * hop % NZ, chunk)].start()
+
+    def wait_pairs(group):
+        for oz in PAIRS[group]:
+            for chunk in range(2):
+                pairs[(oz, chunk)].wait_recv()
 
     def before(step):
         if step == 0:
-            hop(1)
+            relay(1, 0)
             wait_keys(0)
-            pairs[0].wait_recv()
-            pairs[1].wait_recv()
+            share_keys(2)
+            share_keys(3)
+            relay(1, 1)
+            wait_pairs(1)
         if step == 1:
+            relay(2, 0)
             wait_keys(1)
         if step == 2:
-            hop(2)
-            wait_keys(3)
+            relay(2, 1)
+            wait_pairs(2)
         if step == 3:
-            pairs[7].wait_recv()
-            pairs[6].wait_recv()
+            relay(3, 0)
         if step == 4:
-            hop(3)
-        if step == 5:
-            pairs[2].wait_recv()
-            pairs[3].wait_recv()
+            relay(3, 1)
             wait_keys(2)
         if step == 6:
-            rights[3].wait_recv()
-            lefts[3].wait_recv()
-            pairs[4].start()
+            wait_keys(3)
         if step == 7:
-            pairs[4].wait_recv()
-            pairs[5].wait_recv()
+            relay(4, 0)
+            relay(4, 1)
+        if step == 8:
+            wait_pairs(3)
+        if step == 10:
+            wait_pairs(0)
 
     def after(step):
+        if step == 6:
+            swap_queries(1)
         if step == 7:
+            send_queries(1)
+            swap_queries(2)
+        if step == 8:
+            send_queries(2)
+        if step == 10:
+            send_keys(2)
+        if step == 11:
+            send_keys(3)
+        if step == 13:
+            swap_queries(3)
+        if step == 14:
+            send_queries(3)
             send_keys(1)
-        if step == 8:
-            send_keys(3)
-        if step == 10:
-            swap_queries(2)
-        if step == 11:
-            send_queries(2)
-        if step == 12:
-            swap_queries(1)
-        if step == 13:
-            send_queries(1)
+        if step == 15:
             swap_queries(0)
-        if step == 14:
-            send_keys(2)
+            send_keys(0)
             send_queries(0)
-        if step == 15:
-            swap_queries(3)
-            send_keys(0)
-            send_queries(3)
 
     def tile(at_q, at_k):
         first_q, first_k = at_q * 4, at_k * 4
@@ -373,8 +402,8 @@
     for head in range(2):
         part = total[head * DIM : (head + 1) * DIM]
         query_grad[:, pl.ds(head * DIM, DIM)] = part.T.astype(BF16)
-    for offset in plane_offsets:
-        dkv_copies[offset].wait_recv()
+    for slot in range(1, 16):
+        dkv_copies[slot].wait_recv()
     k_total, v_total = dk[0], dv[0]
     for slot in range(1, 16):
         k_total = k_total + dkv_in[slot, 0:DIM].astype(F32)
@@ -382,26 +411,33 @@
     key_grad[...] = (k_total * SCALE).T.astype(BF16)
     value_grad[...] = v_total.T.astype(BF16)
 
-    for copies in (kv_copies, dkv_copies, dq_copies):
+    for copies in (kv_copies, dkv_copies, dq_copies, ring, pairs):
         for copy in copies.values():
             copy.wait_send()
-    for copy in rights + lefts + pairs + sib_copies:
+    for copy in sib_copies:
         copy.wait_send()
+
+
+def finish(q_in, k_in, v_in, q_out, k_out, v_out):
+    q_out[...] = q_in[...]
+    k_out[...] = k_in[...]
+    v_out[...] = v_in[...]
 
 
 def body(query, key, value, out_grad, attn_out, lse, positions):
     vmem = pl.BlockSpec(memory_space=pltpu.VMEM)
     dma = pltpu.SemaphoreType.DMA
-    return pl.pallas_call(
+    parts = pl.pallas_call(
         kernel,
         out_shape=(
             jax.ShapeDtypeStruct((ROWS, 2 * DIM), BF16),
             jax.ShapeDtypeStruct((ROWS, DIM), BF16),
             jax.ShapeDtypeStruct((ROWS, DIM), BF16),
         ),
-        in_specs=[vmem] * 7,
+        in_specs=[vmem] * 6 + [pl.BlockSpec(memory_space=pl.ANY)],
         out_specs=[vmem] * 3,
         scratch_shapes=[
+            pltpu.VMEM((256, ROWS), jnp.int32),
             pltpu.VMEM((16, 4, DIM + AUG, ROWS), BF16),
             pltpu.VMEM((16, REST, ROWS), BF16),
             pltpu.VMEM((16, 2, ROWS, DIM), BF16),
@@ -417,11 +453,12 @@
             pltpu.VMEM((8, 2 * DIM, ROWS), BF16),
             pltpu.VMEM((16, 2 * DIM, ROWS), BF16),
             pltpu.VMEM((16, 2 * DIM, ROWS), BF16),
+            dma,
             dma((16,)),
             dma((16,)),
-            dma((8,)),
-            dma((17,)),
-            dma((8,)),
+            dma((2, 4, 2)),
+            dma((16, 2)),
+            dma((8, 2)),
             dma((8,)),
             dma((8,)),
             dma((8,)),
@@ -432,7 +469,13 @@
         compiler_params=pltpu.CompilerParams(
             collective_id=0, has_side_effects=True, vmem_limit_bytes=56 * 2**20
         ),
-    )(query, key, value, out_grad, attn_out, lse, positions.reshape(256, ROWS))
+    )(query, key, value, out_grad, attn_out, lse.T, positions.reshape(256, ROWS))
+    return pl.pallas_call(
+        finish,
+        out_shape=tuple(jax.ShapeDtypeStruct(part.shape, part.dtype) for part in parts),
+        in_specs=[vmem] * 3,
+        out_specs=[vmem] * 3,
+    )(*parts)
 
 
 def solution(mesh):

time: 65.8 us -> 59.4 us (0.903)
  local copies, waits for them, and re-layouts: 4.28 us -> 0 us
  Pallas kernels: 60.7 us -> 58 us
    unnamed x10 -> x0, local copies, waits for them, and re-layouts: 4.28 us -> none
    pallas_call x1, Pallas kernels: 60.7 us -> 56.4 us  [body(): pl.pallas_call(kernel, out_shape=(jax.ShapeDtypeStruct((ROWS, 2 * DIM), B...]
    pallas_call x0 -> x1, Pallas kernels: none -> 1.51 us  [body(): pl.pallas_call(finish, out_shape=tuple((jax.ShapeDtypeStruct(part.shape,...]
where the time goes in v2:
time: 59.4 us; the launch traced here: 58.6 us
  Pallas kernels  58 us (98%)
  between operations  0.64 us (1%)
    pallas_call x1, Pallas kernels, body(): pl.pallas_call(kernel, out_shape=(jax.ShapeDtypeStruct((ROWS, 2 * DIM), B...  56.4 us
    pallas_call x1, Pallas kernels, body(): pl.pallas_call(finish, out_shape=tuple((jax.ShapeDtypeStruct(part.shape,...  1.51 us

profile of v2, /device:TPU:1, one launch (start us, length us, event | category | flops | bytes accessed | tf_op | source)
XLA Modules:
  0.0 58.6 jit_solution(15917070577606208893)
XLA Ops:
  0.6 56.4 %shard_map.94 = (bf16[128,256]{1,0:T(8,128)(2,1)}, bf16[128,128]{1,0:T(8,128)(2,1)}, bf16[128,128]{1,0:T(8,128)(2,1)}) custom-call(bf16[128,256]{1,0:T(8,128)(2,1)} %query.1, bf16[128,128]{1,0:T(8,128)(2,1)} %key.1, bf16[128,128]{1,0:T(8,128)(2,1)} %value.1, bf16[128,256]{1,0:T(8,128)(2,1)} %out_grad.1, bf16[128,256]{1,0:T(8,128)(2,1)} %attn_out.1, ...), custom_call_target="tpu_custom_call" | custom-call | tf_op jit(solution)/shard_map/pallas_call | solution.py:430
  57.1 1.5 %shard_map.95 = (bf16[128,256]{1,0:T(8,128)(2,1)}, bf16[128,128]{1,0:T(8,128)(2,1)}, bf16[128,128]{1,0:T(8,128)(2,1)}) custom-call(bf16[128,256]{1,0:T(8,128)(2,1)} %get-tuple-element.6.q_in, bf16[128,128]{1,0:T(8,128)(2,1)} %get-tuple-element.7.k_in, bf16[128,128]{1,0:T(8,128)(2,1)} %get-tuple-element.8.v_in), custom_call_target="tpu_custom_call" | custom-call | tf_op jit(solution)/shard_map/pallas_call | solution.py:473

commit v3 on v2

--- a/solution.py
+++ b/solution.py
@@ -30,8 +30,8 @@
 )
 
 TILES = (
-    (1, 0), (1, 1), (2, 0), (2, 1), (1, 2), (2, 2), (1, 3), (2, 3),
-    (3, 2), (3, 3), (0, 2), (0, 3), (3, 1), (3, 0), (0, 1), (0, 0),
+    (0, 1, 0), (0, 1, 1), (0, 2, 0), (0, 2, 1), (0, 1, 2), (0, 2, 2), (0, 1, 3), (0, 2, 3),
+    (0, 3, 2), (0, 3, 3), (0, 0, 2), (0, 0, 3), (0, 3, 1), (0, 3, 0), (0, 0, 1), (0, 0, 0),
 )
 
 
@@ -40,17 +40,6 @@
     for at, value in enumerate(values):
         total += value * 4**at
     return total
-
-
-def place():
-    row, col = lax.axis_index("row"), lax.axis_index("col")
-    x, z_lo, core = col // 8, (col // 2) % 4, col % 2
-    y, z_hi = row // 2, row % 2
-    return x, y, z_hi * 4 + z_lo, core
-
-
-def device(x, y, z, core):
-    return (y * 2 + z // 4, x * 8 + (z % 4) * 2 + core)
 
 
 def kernel(
@@ -63,16 +52,25 @@
 ):
     pos_copy = pltpu.make_async_copy(positions, pos, pos_sem)
     pos_copy.start()
-    x, y, z, core = place()
+    row, col = lax.axis_index("row"), lax.axis_index("col")
+    core = lax.rem(col, 2)
     other = 1 - core
+    x, z_lo = lax.div(col, 8), lax.rem(lax.div(col, 2), 4)
+    y, z_hi = lax.div(row, 2), lax.rem(row, 2)
+    z = z_hi * 4 + z_lo
+    rows_y = [lax.rem(y + oy, NY) * 2 for oy in range(NY)]
+    cols_x = [lax.rem(x + ox, NX) * 8 for ox in range(NX)]
+    zs = [lax.rem(z + oz, NZ) for oz in range(NZ)]
+    rows_z = [lax.div(one, 4) for one in zs]
+    cols_z = [lax.rem(one, 4) * 2 for one in zs]
 
     def plane(ox, oy):
-        return device((x + ox) % NX, (y + oy) % NY, z, core)
+        return (rows_y[oy % NY] + z_hi, cols_x[ox % NX] + (z_lo * 2 + core))
 
     def along(oz, which=None):
-        return device(x, y, (z + oz) % NZ, core if which is None else which)
-
-    sibling = device(x, y, z, other)
+        return (rows_y[0] + rows_z[oz % NZ], cols_x[0] + cols_z[oz % NZ] + (core if which is None else which))
+
+    sibling = (row, col + 1 - 2 * core)
 
     barrier = pltpu.get_barrier_semaphore()
     peers = [plane(ox, oy) for ox, oy in KEY_SPOTS[1:]]
@@ -107,14 +105,15 @@
         return 2 * SPOT[oz % NZ]
 
     def ring_copy(hop, chunk, way):
-        source, target = own_slot(way * (1 - hop)), own_slot(-way * hop)
+        far = max(hop - 2, 1)
+        source, target = own_slot(way * (far - hop)), own_slot(-way * hop)
         cut = pl.ds(2 * chunk, 2)
         return pltpu.make_async_remote_copy(
             src_ref=qd.at[source, cut],
             dst_ref=qd.at[target, cut],
             send_sem=ring_send.at[0 if way > 0 else 1, hop - 1, chunk],
             recv_sem=q_recv.at[target, chunk],
-            device_id=along(way % NZ),
+            device_id=along(way * far),
             device_id_type=MESH,
         )
 
@@ -144,18 +143,35 @@
         return pltpu.make_async_remote_copy(
             src_ref=kv.at[0],
             dst_ref=kv.at[slot],
-            send_sem=kv_send.at[slot],
-            recv_sem=kv_recv.at[slot],
-            device_id=plane(NX - ox, NY - oy),
-            device_id_type=MESH,
-        )
-
-    kv_copies = {slot: kv_copy(slot) for slot in range(1, 16)}
+            send_sem=kv_send.at[slot, 0],
+            recv_sem=kv_recv.at[slot, 0],
+            device_id=plane(-ox, -oy),
+            device_id_type=MESH,
+        )
+
+    def kv_relay(slot, part):
+        ox, oy = KEY_SPOTS[slot]
+        middle = KEY_SPOTS.index((0, oy) if part else (ox, 0))
+        return pltpu.make_async_remote_copy(
+            src_ref=kv.at[middle, part],
+            dst_ref=kv.at[slot, part],
+            send_sem=kv_send.at[slot, part],
+            recv_sem=kv_recv.at[slot, part],
+            device_id=plane(-ox, 0) if part else plane(0, -oy),
+            device_id_type=MESH,
+        )
+
+    kv_copies = {slot: kv_copy(slot) for slot in range(1, 8)}
+    kv_relays = {(slot, part): kv_relay(slot, part) for slot in range(8, 16) for part in range(2)}
 
     def share_keys(group):
         for slot in range(4 * group, 4 * group + 4):
             if slot:
                 kv_copies[slot].start()
+
+    def relay_keys(part):
+        for slot in range(8, 16):
+            kv_relays[(slot, part)].start()
 
     for chunk in range(2):
         for way in (1, -1):
@@ -202,15 +218,19 @@
     inside = (at_key <= at_row) & (at_key // 64 == at_row // 64)
     probs = jnp.where(inside, jnp.exp2(scores * EXP_SCALE), 0.0)
     dscores = (probs * dprobs).astype(BF16)
-    dv[0] = lax.dot_general(d_cat[:DIM], probs.astype(BF16), NT, preferred_element_type=F32)
-    dk[0] = lax.dot_general(q_cat[:DIM], dscores, NT, preferred_element_type=F32)
+    dv[0] = lax.dot_general(probs.astype(BF16), d_cat[:DIM], NT, preferred_element_type=F32)
+    dk[0] = lax.dot_general(dscores, q_cat[:DIM], NT, preferred_element_type=F32)
     part = jnp.dot(kt[0], dscores, preferred_element_type=F32)
     dq[0] = jnp.concatenate([part[:, :ROWS], part[:, ROWS:]], 0)
 
     def wait_keys(group):
         for slot in range(4 * group, 4 * group + 4):
+            if slot in kv_copies:
+                kv_copies[slot].wait_recv()
+            if (slot, 0) in kv_relays:
+                kv_relays[(slot, 0)].wait_recv()
+                kv_relays[(slot, 1)].wait_recv()
             if slot:
-                kv_copies[slot].wait_recv()
                 turn(slot)
 
     def dkv_copy(slot):
@@ -256,13 +276,13 @@
 
     dq_copies = {oz: dq_copy(oz) for oz in range(1, NZ)}
 
-    def swap_queries(group):
-        for oz in PAIRS[group]:
+    def swap_queries(*offsets):
+        for oz in offsets:
             sib_out[oz] = dq[own_slot(oz) + 1].astype(BF16)
             sib_copies[oz].start()
 
-    def send_queries(group):
-        for oz in PAIRS[group]:
+    def send_queries(*offsets):
+        for oz in offsets:
             sib_copies[oz].wait_recv()
             total = dq[own_slot(oz)] + sib_in[oz].astype(F32)
             if oz:
@@ -275,81 +295,86 @@
         for way in (1, -1):
             if (hop, chunk, way) in ring:
                 ring[(hop, chunk, way)].wait_recv()
-                if (hop + 1, chunk, way) in ring:
-                    ring[(hop + 1, chunk, way)].start()
+                for later in {1: (2,), 2: (3, 4)}.get(hop, ()):
+                    if (later, chunk, way) in ring:
+                        ring[(later, chunk, way)].start()
                 pairs[(-way * hop % NZ, chunk)].start()
 
-    def wait_pairs(group):
-        for oz in PAIRS[group]:
+    def wait_pairs(*offsets):
+        for oz in offsets:
             for chunk in range(2):
                 pairs[(oz, chunk)].wait_recv()
 
     def before(step):
         if step == 0:
             relay(1, 0)
+            relay(1, 1)
             wait_keys(0)
-            share_keys(2)
-            share_keys(3)
-            relay(1, 1)
-            wait_pairs(1)
+            relay_keys(0)
+            wait_pairs(1, 7)
         if step == 1:
+            wait_keys(1)
+            relay_keys(1)
             relay(2, 0)
-            wait_keys(1)
         if step == 2:
             relay(2, 1)
-            wait_pairs(2)
-        if step == 3:
+            wait_pairs(2, 6)
+        if step == 4:
+            wait_keys(2)
+        if step == 5:
             relay(3, 0)
-        if step == 4:
+        if step == 6:
             relay(3, 1)
-            wait_keys(2)
-        if step == 6:
             wait_keys(3)
         if step == 7:
             relay(4, 0)
             relay(4, 1)
         if step == 8:
-            wait_pairs(3)
+            wait_pairs(3, 5)
         if step == 10:
-            wait_pairs(0)
+            wait_pairs(0, 4)
 
     def after(step):
         if step == 6:
-            swap_queries(1)
+            swap_queries(1, 7)
         if step == 7:
-            send_queries(1)
-            swap_queries(2)
+            send_queries(1, 7)
+            swap_queries(2, 6)
         if step == 8:
-            send_queries(2)
+            send_queries(2, 6)
         if step == 10:
             send_keys(2)
         if step == 11:
             send_keys(3)
         if step == 13:
-            swap_queries(3)
+            swap_queries(3, 5)
         if step == 14:
-            send_queries(3)
+            send_queries(3, 5)
             send_keys(1)
         if step == 15:
-            swap_queries(0)
+            swap_queries(4, 0)
             send_keys(0)
-            send_queries(0)
-
-    def tile(at_q, at_k):
-        first_q, first_k = at_q * 4, at_k * 4
-        marks = ka[pl.ds(first_k, 4)].reshape(4 * ROWS, ROWS)
-        k_part = kv[pl.ds(first_k, 4), 0].reshape(4 * ROWS, DIM)
-        v_part = kv[pl.ds(first_k, 4), 1].reshape(4 * ROWS, DIM)
+            send_queries(4, 0)
+
+    def between(step):
+        if step:
+            after(step - 1)
+        before(step)
+
+    def tile(first_q, n_q, first_k, n_k):
+        marks = ka[pl.ds(first_k, n_k)].reshape(n_k * ROWS, ROWS)
+        k_part = kv[pl.ds(first_k, n_k), 0].reshape(n_k * ROWS, DIM)
+        v_part = kv[pl.ds(first_k, n_k), 1].reshape(n_k * ROWS, DIM)
         k_wide = jnp.concatenate([k_part, marks], 1)
         v_wide = jnp.concatenate([v_part, marks], 1)
         q_cols = [
             jnp.concatenate([qd[first_q + a, head], qm[first_q + a]], 0)
-            for a in range(4)
+            for a in range(n_q)
             for head in range(2)
         ]
         d_cols = [
             jnp.concatenate([qd[first_q + a, 2 + head], none], 0)
-            for a in range(4)
+            for a in range(n_q)
             for head in range(2)
         ]
         q_wide = jnp.concatenate(q_cols, 1)
@@ -359,39 +384,45 @@
         probs = jnp.exp2(scores * EXP_SCALE)
         dscores = (probs * dprobs).astype(BF16)
         v_sum = lax.dot_general(
-            d_wide[:DIM], probs.astype(BF16), NT, preferred_element_type=F32
-        )
-        k_sum = lax.dot_general(q_wide[:DIM], dscores, NT, preferred_element_type=F32)
-        k_turned = jnp.concatenate([kt[first_k + a] for a in range(4)], 1)
+            probs.astype(BF16), d_wide[:DIM], NT, preferred_element_type=F32
+        )
+        k_sum = lax.dot_general(dscores, q_wide[:DIM], NT, preferred_element_type=F32)
+        k_turned = jnp.concatenate([kt[first_k + a] for a in range(n_k)], 1)
         q_sum = jnp.dot(k_turned, dscores, preferred_element_type=F32)
-        for a in range(4):
-            dv[first_k + a] += v_sum[:, a * ROWS : (a + 1) * ROWS]
-            dk[first_k + a] += k_sum[:, a * ROWS : (a + 1) * ROWS]
+        for a in range(n_k):
+            dv[first_k + a] += v_sum[a * ROWS : (a + 1) * ROWS]
+            dk[first_k + a] += k_sum[a * ROWS : (a + 1) * ROWS]
+        for a in range(n_q):
             for head in range(2):
                 col = (2 * a + head) * ROWS
                 dq[first_q + a, pl.ds(head * DIM, DIM)] += q_sum[:, col : col + ROWS]
 
-    q_tables = [table(q for q, _ in TILES[8 * half : 8 * half + 8]) for half in range(2)]
-    k_tables = [table(k for _, k in TILES[8 * half : 8 * half + 8]) for half in range(2)]
+    tables = [
+        [table(entry[part] for entry in TILES[8 * half : 8 * half + 8]) for part in range(3)]
+        for half in range(2)
+    ]
 
     def run_half(half, carry):
-        q_list = q_tables[0] + half * (q_tables[1] - q_tables[0])
-        k_list = k_tables[0] + half * (k_tables[1] - k_tables[0])
+        lists = tuple(one + half * (two - one) for one, two in zip(*tables))
 
         def run_tile(at, lists):
-            q_list, k_list = lists
+            _, q_part, k_part = (one % 4 for one in lists)
             step = half * 8 + at
-            for n in range(16):
-                pl.when(step == n)(functools.partial(before, n))
-            tile(q_list % 4, k_list % 4)
-            for n in range(16):
-                pl.when(step == n)(functools.partial(after, n))
-            return q_list // 4, k_list // 4
-
-        lax.fori_loop(0, 8, run_tile, (q_list, k_list))
+            for part in range(4):
+
+                @pl.when(at // 2 == part)
+                def _():
+                    for n in (2 * part, 2 * part + 1, 2 * part + 8, 2 * part + 9):
+                        pl.when(step == n)(functools.partial(between, n))
+
+            tile(q_part * 4, 4, k_part * 4, 4)
+            return tuple(one // 4 for one in lists)
+
+        lax.fori_loop(0, 8, run_tile, lists)
         return carry
 
     lax.fori_loop(0, 2, run_half, 0)
+    after(15)
 
     for oz in range(1, NZ):
         dq_copies[oz].wait_recv()
@@ -408,10 +439,10 @@
     for slot in range(1, 16):
         k_total = k_total + dkv_in[slot, 0:DIM].astype(F32)
         v_total = v_total + dkv_in[slot, DIM:].astype(F32)
-    key_grad[...] = (k_total * SCALE).T.astype(BF16)
-    value_grad[...] = v_total.T.astype(BF16)
-
-    for copies in (kv_copies, dkv_copies, dq_copies, ring, pairs):
+    key_grad[...] = (k_total * SCALE).astype(BF16)
+    value_grad[...] = v_total.astype(BF16)
+
+    for copies in (kv_copies, kv_relays, dkv_copies, dq_copies, ring, pairs):
         for copy in copies.values():
             copy.wait_send()
     for copy in sib_copies:
@@ -454,8 +485,8 @@
             pltpu.VMEM((16, 2 * DIM, ROWS), BF16),
             pltpu.VMEM((16, 2 * DIM, ROWS), BF16),
             dma,
-            dma((16,)),
-            dma((16,)),
+            dma((16, 2)),
+            dma((16, 2)),
             dma((2, 4, 2)),
             dma((16, 2)),
             dma((8, 2)),

time: 59.4 us -> 58.1 us (0.978); the launches traced: 58.6 us -> 58 us
  Pallas kernels: 58 us -> 57.3 us
    pallas_call x1, Pallas kernels: 56.4 us -> 55.8 us  [body(): pl.pallas_call(kernel, out_shape=(jax.ShapeDtypeStruct((ROWS, 2 * DIM), B...]
where the time goes in v3:
time: 58.1 us; the launch traced here: 58 us
  Pallas kernels  57.3 us (99%)
  between operations  0.64 us (1%)
    pallas_call x1, Pallas kernels, body(): pl.pallas_call(kernel, out_shape=(jax.ShapeDtypeStruct((ROWS, 2 * DIM), B...  55.8 us
    pallas_call x1, Pallas kernels, body(): pl.pallas_call(finish, out_shape=tuple((jax.ShapeDtypeStruct(part.shape,...  1.51 us

profile of v3, /device:TPU:1, one launch (start us, length us, event | category | flops | bytes accessed | tf_op | source)
XLA Modules:
  0.0 58.0 jit_solution(6729629723572300802)
XLA Ops:
  0.6 55.8 %shard_map.94 = (bf16[128,256]{1,0:T(8,128)(2,1)}, bf16[128,128]{1,0:T(8,128)(2,1)}, bf16[128,128]{1,0:T(8,128)(2,1)}) custom-call(bf16[128,256]{1,0:T(8,128)(2,1)} %query.1, bf16[128,128]{1,0:T(8,128)(2,1)} %key.1, bf16[128,128]{1,0:T(8,128)(2,1)} %value.1, bf16[128,256]{1,0:T(8,128)(2,1)} %out_grad.1, bf16[128,256]{1,0:T(8,128)(2,1)} %attn_out.1, ...), custom_call_target="tpu_custom_call" | custom-call | tf_op jit(solution)/shard_map/pallas_call | solution.py:461
  56.5 1.5 %shard_map.95 = (bf16[128,256]{1,0:T(8,128)(2,1)}, bf16[128,128]{1,0:T(8,128)(2,1)}, bf16[128,128]{1,0:T(8,128)(2,1)}) custom-call(bf16[128,256]{1,0:T(8,128)(2,1)} %get-tuple-element.6.q_in, bf16[128,128]{1,0:T(8,128)(2,1)} %get-tuple-element.7.k_in, bf16[128,128]{1,0:T(8,128)(2,1)} %get-tuple-element.8.v_in), custom_call_target="tpu_custom_call" | custom-call | tf_op jit(solution)/shard_map/pallas_call | solution.py:504

commit v4 on v3

--- a/solution.py
+++ b/solution.py
@@ -48,7 +48,7 @@
     pos, qd, qm, kv, kt, ka, kp, dq, dk, dv,
     sib_out, sib_in, dq_out, dq_in, dkv_out, dkv_in,
     pos_sem, kv_send, kv_recv, ring_send, q_recv, pair_send,
-    sib_send, sib_recv, dq_send, dq_recv, dkv_send, dkv_recv,
+    sib_send, sib_recv, dq_send, dq_recv, dkv_send, dkv_recv, met,
 ):
     pos_copy = pltpu.make_async_copy(positions, pos, pos_sem)
     pos_copy.start()
@@ -73,10 +73,14 @@
     sibling = (row, col + 1 - 2 * core)
 
     barrier = pltpu.get_barrier_semaphore()
-    peers = [plane(ox, oy) for ox, oy in KEY_SPOTS[1:]]
-    peers += [along(oz) for oz in range(1, NZ)] + [sibling]
-    for peer in peers:
+    near = [along(1), along(-1), plane(1, 0), plane(-1, 0), plane(0, 1), plane(0, -1), sibling]
+    for peer in near:
         pl.semaphore_signal(barrier, inc=1, device_id=peer, device_id_type=MESH)
+
+    def greet(turn):
+        for peer in near:
+            pl.semaphore_signal(met.at[turn], inc=1, device_id=peer, device_id_type=MESH)
+
 
     kv[0, 0] = key[...]
     kv[0, 1] = value[...]
@@ -99,7 +103,7 @@
         qd[0, 2 + head, 0:DIM] = grads.T
         qd[0, 2 + head, DIM : DIM + AUG] = split_rows(-delta)
 
-    pl.semaphore_wait(barrier, len(peers))
+    pl.semaphore_wait(barrier, len(near))
 
     def own_slot(oz):
         return 2 * SPOT[oz % NZ]
@@ -164,11 +168,6 @@
     kv_copies = {slot: kv_copy(slot) for slot in range(1, 8)}
     kv_relays = {(slot, part): kv_relay(slot, part) for slot in range(8, 16) for part in range(2)}
 
-    def share_keys(group):
-        for slot in range(4 * group, 4 * group + 4):
-            if slot:
-                kv_copies[slot].start()
-
     def relay_keys(part):
         for slot in range(8, 16):
             kv_relays[(slot, part)].start()
@@ -176,10 +175,11 @@
     for chunk in range(2):
         for way in (1, -1):
             ring[(1, chunk, way)].start()
-    share_keys(0)
-    share_keys(1)
+    for slot in (1, 2, 4, 5):
+        kv_copies[slot].start()
     for chunk in range(2):
         pairs[(0, chunk)].start()
+    greet(0)
     pos_copy.wait()
 
     dq[...] = jnp.zeros_like(dq)
@@ -200,6 +200,11 @@
         bias = jnp.where(kp[...] < places, 0.0, FAR)
         qm[slot] = jnp.concatenate([bias, jnp.zeros((REST - 32, ROWS), F32)], 0).astype(BF16)
 
+    pl.semaphore_wait(met.at[0], len(near))
+    for slot in (3, 6, 7):
+        kv_copies[slot].start()
+    greet(1)
+
     none = jnp.zeros((REST, ROWS), BF16)
 
     def turn(slot):
@@ -316,12 +321,15 @@
             wait_keys(1)
             relay_keys(1)
             relay(2, 0)
+            pl.semaphore_wait(met.at[1], len(near))
+            greet(2)
         if step == 2:
             relay(2, 1)
             wait_pairs(2, 6)
         if step == 4:
             wait_keys(2)
         if step == 5:
+            pl.semaphore_wait(met.at[2], len(near))
             relay(3, 0)
         if step == 6:
             relay(3, 1)
@@ -496,6 +504,7 @@
             dma((8,)),
             dma((16,)),
             dma((16,)),
+            pltpu.SemaphoreType.REGULAR((3,)),
         ],
         compiler_params=pltpu.CompilerParams(
             collective_id=0, has_side_effects=True, vmem_limit_bytes=56 * 2**20

time: 58.1 us -> 56 us (0.964)
  Pallas kernels: 57.3 us -> 55.1 us
    pallas_call x1, Pallas kernels: 55.8 us -> 53.6 us  [body(): pl.pallas_call(kernel, out_shape=(jax.ShapeDtypeStruct((ROWS, 2 * DIM), B...]
where the time goes in v4:
time: 56 us; the launch traced here: 55.8 us
  Pallas kernels  55.1 us (98%)
  between operations  0.64 us (1%)
    pallas_call x1, Pallas kernels, body(): pl.pallas_call(kernel, out_shape=(jax.ShapeDtypeStruct((ROWS, 2 * DIM), B...  53.6 us
    pallas_call x1, Pallas kernels, body(): pl.pallas_call(finish, out_shape=tuple((jax.ShapeDtypeStruct(part.shape,...  1.51 us

profile of v4, /device:TPU:1, one launch (start us, length us, event | category | flops | bytes accessed | tf_op | source)
XLA Modules:
  0.0 55.8 jit_solution(660442515084458659)
XLA Ops:
  0.6 53.6 %shard_map.94 = (bf16[128,256]{1,0:T(8,128)(2,1)}, bf16[128,128]{1,0:T(8,128)(2,1)}, bf16[128,128]{1,0:T(8,128)(2,1)}) custom-call(bf16[128,256]{1,0:T(8,128)(2,1)} %query.1, bf16[128,128]{1,0:T(8,128)(2,1)} %key.1, bf16[128,128]{1,0:T(8,128)(2,1)} %value.1, bf16[128,256]{1,0:T(8,128)(2,1)} %out_grad.1, bf16[128,256]{1,0:T(8,128)(2,1)} %attn_out.1, ...), custom_call_target="tpu_custom_call" | custom-call | tf_op jit(solution)/shard_map/pallas_call | solution.py:469
  54.3 1.5 %shard_map.95 = (bf16[128,256]{1,0:T(8,128)(2,1)}, bf16[128,128]{1,0:T(8,128)(2,1)}, bf16[128,128]{1,0:T(8,128)(2,1)}) custom-call(bf16[128,256]{1,0:T(8,128)(2,1)} %get-tuple-element.6.q_in, bf16[128,128]{1,0:T(8,128)(2,1)} %get-tuple-element.7.k_in, bf16[128,128]{1,0:T(8,128)(2,1)} %get-tuple-element.8.v_in), custom_call_target="tpu_custom_call" | custom-call | tf_op jit(solution)/shard_map/pallas_call | solution.py:513

commit v5 on v4

--- a/solution.py
+++ b/solution.py
@@ -205,6 +205,18 @@
         kv_copies[slot].start()
     greet(1)
 
+    def relay(hop, chunk):
+        for way in (1, -1):
+            if (hop, chunk, way) in ring:
+                ring[(hop, chunk, way)].wait_recv()
+                for later in {1: (2,), 2: (3, 4)}.get(hop, ()):
+                    if (later, chunk, way) in ring:
+                        ring[(later, chunk, way)].start()
+                pairs[(-way * hop % NZ, chunk)].start()
+
+    relay(1, 0)
+    relay(1, 1)
+
     none = jnp.zeros((REST, ROWS), BF16)
 
     def turn(slot):
@@ -296,15 +308,6 @@
             else:
                 dq[0] = total
 
-    def relay(hop, chunk):
-        for way in (1, -1):
-            if (hop, chunk, way) in ring:
-                ring[(hop, chunk, way)].wait_recv()
-                for later in {1: (2,), 2: (3, 4)}.get(hop, ()):
-                    if (later, chunk, way) in ring:
-                        ring[(later, chunk, way)].start()
-                pairs[(-way * hop % NZ, chunk)].start()
-
     def wait_pairs(*offsets):
         for oz in offsets:
             for chunk in range(2):
@@ -312,8 +315,6 @@
 
     def before(step):
         if step == 0:
-            relay(1, 0)
-            relay(1, 1)
             wait_keys(0)
             relay_keys(0)
             wait_pairs(1, 7)

time: 56 us -> 56 us (level)
  no operation moved by 1% of the time
where the time goes in v5:
time: 56 us; the launch traced here: 55.8 us
  Pallas kernels  55.1 us (98%)
  between operations  0.64 us (1%)
    pallas_call x1, Pallas kernels, body(): pl.pallas_call(kernel, out_shape=(jax.ShapeDtypeStruct((ROWS, 2 * DIM), B...  53.6 us
    pallas_call x1, Pallas kernels, body(): pl.pallas_call(finish, out_shape=tuple((jax.ShapeDtypeStruct(part.shape,...  1.51 us

profile of v5, /device:TPU:1, one launch (start us, length us, event | category | flops | bytes accessed | tf_op | source)
XLA Modules:
  0.0 55.8 jit_solution(17821953833819664887)
XLA Ops:
  0.6 53.6 %shard_map.94 = (bf16[128,256]{1,0:T(8,128)(2,1)}, bf16[128,128]{1,0:T(8,128)(2,1)}, bf16[128,128]{1,0:T(8,128)(2,1)}) custom-call(bf16[128,256]{1,0:T(8,128)(2,1)} %query.1, bf16[128,128]{1,0:T(8,128)(2,1)} %key.1, bf16[128,128]{1,0:T(8,128)(2,1)} %value.1, bf16[128,256]{1,0:T(8,128)(2,1)} %out_grad.1, bf16[128,256]{1,0:T(8,128)(2,1)} %attn_out.1, ...), custom_call_target="tpu_custom_call" | custom-call | tf_op jit(solution)/shard_map/pallas_call | solution.py:470
  54.3 1.5 %shard_map.95 = (bf16[128,256]{1,0:T(8,128)(2,1)}, bf16[128,128]{1,0:T(8,128)(2,1)}, bf16[128,128]{1,0:T(8,128)(2,1)}) custom-call(bf16[128,256]{1,0:T(8,128)(2,1)} %get-tuple-element.6.q_in, bf16[128,128]{1,0:T(8,128)(2,1)} %get-tuple-element.7.k_in, bf16[128,128]{1,0:T(8,128)(2,1)} %get-tuple-element.8.v_in), custom_call_target="tpu_custom_call" | custom-call | tf_op jit(solution)/shard_map/pallas_call | solution.py:514
